TPU v7x, 256 devices: a whole 4x4x8 slice. The times are simulated.
256 devices in a mesh: dp: 16 (over z, x_hi), ctx: 16 (over y, x_lo, core).
Axes of the slice: x: 4 (x_hi: 2, x_lo: 2; x = x_hi * 2 + x_lo), y: 4, z: 8, core: 2. Of those that a mesh axis runs over, the one named last changes fastest.
Arguments:
- query_rows: bfloat16 [16, 3584, 1024], P('dp', 'ctx'), may hold values from -48 to 48
- key_rows: bfloat16 [16, 3584, 128], P('dp', 'ctx'), may hold values from -4 to 4
- value_rows: bfloat16 [16, 3584, 128], P('dp', 'ctx'), may hold values from -5 to 5
- out_grad: bfloat16 [16, 3584, 1024], P('dp', 'ctx'), may hold values from -5 to 5
- doc_ids: int32 [16, 3584], P('dp'), may hold values from 0 to 7, never falling along the last dimension, each value on 1 to 2688 neighbouring positions
- matching: int32 [16], replicated, may hold values from 0 to 15, as said below
Outputs:
- attended: bfloat16 [16, 3584, 1024], P('dp', 'ctx')
- query_grad: bfloat16 [16, 3584, 1024], P('dp', 'ctx')
- key_grad: bfloat16 [16, 3584, 128], P('dp', 'ctx')
- value_grad: bfloat16 [16, 3584, 128], P('dp', 'ctx')
Inputs may be any that keep to these rules, and one draw needn't show every extreme that they name: matching[b] is b XOR m for one m of 1 to 15 shared by all b, so micro-batches come in pairs.
All inputs are finite; a program needn't handle non-finite values.
Results may differ from a plain program's by a relative error of at most 0.035.
Values may be sent and summed in bfloat16 or wider, within the bound.
No kernel may reach another device: no remote copies, remote signals or barrier semaphores. Data moves between devices by JAX's collectives and lax.ppermute only.
A program may use at most 64 MiB of HBM per device.

v0:
```python
import functools
import math

import jax
import jax.numpy as jnp
from jax import lax
from jax.experimental import pallas as pl
from jax.experimental.pallas import tpu as pltpu
from jax.sharding import PartitionSpec as P

TILE = 512
LANES = 256


def dot(a, b, ca, cb):
    return lax.dot_general(a, b, (((ca,), (cb,)), ((), ())), preferred_element_type=jnp.float32)


def attention_kernel(
    heads, width, span, scale,
    device, docs, query, grad, gathered,
    out, dquery, terms,
    q_rows, g_rows, o_rows, g_cols, pairs, dpairs, scores, weights, dscores, out_t, dq_t, top, total, low,
    in_sem, pair_sem, out_sem,
):
    rows = heads * span
    keys = pairs.shape[0]
    chunks = [slice(r, r + LANES) for r in range(0, rows, LANES)]
    me = device[0]
    offset = me * span
    factor = scale * math.log2(math.e)

    def head_copies(wide, stacked, sem, to_stacked):
        made = []
        for h in range(heads):
            a = wide.at[:, h * width : (h + 1) * width]
            b = stacked.at[h * span : (h + 1) * span, :]
            a, b = (a, b) if to_stacked else (b, a)
            made.append(pltpu.make_async_copy(a, b, sem.at[h]))
        return made

    own_q = head_copies(query, q_rows, in_sem.at[0], True)
    own_g = head_copies(grad, g_rows, in_sem.at[1], True)
    pair_in = pltpu.make_async_copy(gathered, pairs, pair_sem.at[0])
    for c in own_q + [pair_in] + own_g:
        c.start()

    names = docs[...]
    row = pltpu.roll(names, lax.rem(keys - offset, keys), 1)[:, 0:span]
    start = jnp.zeros((1, span), jnp.int32)
    for d in range(1, 8):
        before = jnp.sum((names < d).astype(jnp.int32), axis=1, keepdims=True)
        start = jnp.where(row == d, before, start)
    place = offset + lax.broadcasted_iota(jnp.int32, (1, span), 1)
    for h in range(heads):
        low[0:1, h * span : (h + 1) * span] = start
        low[1:2, h * span : (h + 1) * span] = place
    low_first, low_last = jnp.min(start), jnp.max(start)
    end = offset + span
    count = lax.div(end - low_first + TILE - 1, TILE)
    base = jnp.maximum(end - count * TILE, 0)
    clear = jnp.minimum(lax.div(jnp.maximum(low_last - base, 0) + TILE - 1, TILE), count)
    full = jnp.minimum(jnp.maximum(lax.div(offset + 1 - base, TILE), clear), count)

    top[...] = jnp.full(top.shape, -jnp.inf, jnp.float32)
    total[...] = jnp.zeros(total.shape, jnp.float32)
    out_t[...] = jnp.zeros(out_t.shape, jnp.float32)
    dq_t[...] = jnp.zeros(dq_t.shape, jnp.float32)
    dpairs[...] = jnp.zeros(dpairs.shape, jnp.bfloat16)
    for c in own_q + [pair_in]:
        c.wait()

    def keys_at(t):
        return pl.ds(pl.multiple_of(base + t * TILE, 32), TILE)

    def kept_at(t):
        return pl.ds(pl.multiple_of(t * TILE, TILE), TILE)

    def score_tile(t, masked):
        key = pairs[keys_at(t), 0:width]
        for c in chunks:
            s = dot(key, q_rows[c, :], 1, 1)
            if masked:
                place = base + t * TILE + lax.broadcasted_iota(jnp.int32, (TILE, LANES), 0)
                ok = (place >= low[0:1, c]) & (place <= low[1:2, c])
                s = jnp.where(ok, s, -jnp.inf)
            scores[kept_at(t), c] = s
            top[:, c] = jnp.maximum(top[:, c], jnp.max(s.reshape(TILE // 8, 8, LANES), axis=0))

    @pl.loop(0, clear)
    def _(t):
        score_tile(t, True)

    @pl.loop(clear, full)
    def _(t):
        score_tile(t, False)

    @pl.loop(full, count)
    def _(t):
        score_tile(t, True)

    peak = jnp.max(top[...], axis=0, keepdims=True) * factor
    top[...] = jnp.broadcast_to(peak, top.shape)

    @pl.loop(0, count)
    def _(t):
        value_t = pairs[keys_at(t), width : 2 * width].T
        for c in chunks:
            p = jnp.exp2(scores[kept_at(t), c] * factor - top[0:1, c])
            total[:, c] += jnp.sum(p.reshape(TILE // 8, 8, LANES), axis=0)
            weights[kept_at(t), c] = p.astype(jnp.bfloat16)
        out_t[...] += dot(value_t, weights[kept_at(t), :], 1, 0)

    for c in own_g:
        c.wait()
    inverse = 1.0 / jnp.sum(total[...], axis=0, keepdims=True)
    for r in range(0, rows, 128):
        c = slice(r, r + 128)
        o = out_t[:, c] * inverse[:, c]
        g = (g_rows[c, :].T.astype(jnp.float32) * inverse[:, c]).astype(jnp.bfloat16)
        g_cols[:, c] = g
        top[0:1, c] = jnp.sum(g.astype(jnp.float32) * o, axis=0, keepdims=True)
        o_rows[c, :] = o.T.astype(jnp.bfloat16)
    out_copies = head_copies(out, o_rows, out_sem.at[0], False)
    for c in out_copies:
        c.start()

    @pl.loop(0, count)
    def _(t):
        at = keys_at(t)
        kept = kept_at(t)
        key = pairs[at, 0:width]
        key_t = key.T
        value = pairs[at, width : 2 * width]
        dv = dot(weights[kept, :], g_cols[...], 1, 1)
        dpairs[at, width : 2 * width] = dv.astype(jnp.bfloat16)
        for c in chunks:
            dp = dot(value, g_cols[:, c], 1, 0)
            dscores[:, c] = weights[kept, c] * (dp - top[0:1, c]).astype(jnp.bfloat16)
        dk = dot(dscores[...], q_rows[...], 1, 0)
        dpairs[at, 0:width] = (dk * scale).astype(jnp.bfloat16)
        dq_t[...] += dot(key_t, dscores[...], 1, 0)

    pair_out = pltpu.make_async_copy(dpairs, terms, pair_sem.at[1])
    pair_out.start()
    for r in range(0, rows, 128):
        g_rows[r : r + 128, :] = (dq_t[:, r : r + 128].T * scale).astype(jnp.bfloat16)
    last_copies = head_copies(dquery, g_rows, out_sem.at[1], False)
    for c in last_copies:
        c.start()
    for c in out_copies + [pair_out] + last_copies:
        c.wait()


def attention(device, docs, query, grad, gathered, width):
    span, features = query.shape
    heads = features // width
    rows, keys = heads * span, gathered.shape[0]
    kernel = functools.partial(attention_kernel, heads, width, span, 1.0 / math.sqrt(width))
    vmem, hbm = pl.BlockSpec(memory_space=pltpu.VMEM), pl.BlockSpec(memory_space=pl.ANY)
    bf16, f32 = jnp.bfloat16, jnp.float32
    return pl.pallas_call(
        kernel,
        out_shape=(
            jax.ShapeDtypeStruct((span, features), bf16),
            jax.ShapeDtypeStruct((span, features), bf16),
            jax.ShapeDtypeStruct(gathered.shape, bf16),
        ),
        in_specs=[pl.BlockSpec(memory_space=pltpu.SMEM), vmem] + [hbm] * 3,
        out_specs=(hbm,) * 3,
        scratch_shapes=[
            pltpu.VMEM((rows, width), bf16),
            pltpu.VMEM((rows, width), bf16),
            pltpu.VMEM((rows, width), bf16),
            pltpu.VMEM((width, rows), bf16),
            pltpu.VMEM((keys, 2 * width), bf16),
            pltpu.VMEM((keys, 2 * width), bf16),
            pltpu.VMEM((keys, rows), f32),
            pltpu.VMEM((keys, rows), bf16),
            pltpu.VMEM((TILE, rows), bf16),
            pltpu.VMEM((width, rows), f32),
            pltpu.VMEM((width, rows), f32),
            pltpu.VMEM((8, rows), f32),
            pltpu.VMEM((8, rows), f32),
            pltpu.VMEM((8, rows), jnp.int32),
            pltpu.SemaphoreType.DMA((2, heads)),
            pltpu.SemaphoreType.DMA((2,)),
            pltpu.SemaphoreType.DMA((2, heads)),
        ],
        compiler_params=pltpu.CompilerParams(vmem_limit_bytes=58 * 1024 * 1024),
        cost_estimate=pl.CostEstimate(
            flops=12 * rows * keys * width // 2, bytes_accessed=6 << 20, transcendentals=rows * keys // 2
        ),
        name="attention",
    )(device, docs, query, grad, gathered)


def across(block, matching, dp_size):
    def turn(mask):
        return lambda v: lax.ppermute(v, "dp", [(i, i ^ mask) for i in range(dp_size)])

    return lax.switch(matching[0] - 1, [turn(mask) for mask in range(1, dp_size)], block)


def on_device(query_rows, key_rows, value_rows, out_grad, doc_ids, matching):
    ctx_size, dp_size = lax.axis_size("ctx"), lax.axis_size("dp")
    me = lax.axis_index("ctx")
    span, width = key_rows.shape[1:]
    is_last = me == ctx_size - 1
    stored = jnp.concatenate([key_rows[0], value_rows[0]], axis=1)
    names = doc_ids.astype(jnp.bfloat16).reshape(-1, 2 * width)
    names = jnp.pad(names, ((0, -names.shape[0] % 16), (0, 0)))
    arrived = across(jnp.concatenate([stored, names], axis=0), matching, dp_size)
    to_last = jnp.where(is_last, stored, arrived[:span])
    sending = jnp.concatenate(
        [jnp.broadcast_to(stored[None], (ctx_size - 1,) + stored.shape), to_last[None]], axis=0
    )
    gathered = lax.all_to_all(sending, "ctx", 0, 0).reshape(ctx_size * span, 2 * width)
    count = doc_ids.shape[1] // (2 * width)
    far = arrived[span : span + count].reshape(1, -1).astype(jnp.int32)
    docs = jnp.where(is_last, far, doc_ids)
    out, dquery, terms = attention(
        me.astype(jnp.int32)[None], docs, query_rows[0], out_grad[0], gathered, width
    )
    terms = lax.all_to_all(terms.reshape(ctx_size, span, 2 * width), "ctx", 0, 0)
    tail = terms[ctx_size - 1]
    back = across(tail, matching, dp_size).astype(jnp.float32)
    own = jnp.sum(terms[: ctx_size - 1].astype(jnp.float32), axis=0)
    final = jnp.where(is_last, tail.astype(jnp.float32), own + back).astype(jnp.bfloat16)
    return out[None], dquery[None], final[None, :, :width], final[None, :, width:]


def solution(mesh):
    rows = P("dp", "ctx", None)
    return jax.shard_map(
        on_device,
        mesh=mesh,
        in_specs=(rows, rows, rows, rows, P("dp", None), P()),
        out_specs=(rows, rows, rows, rows),
        check_vma=False,
    )
```

profile of v0, /device:TPU:2, one launch (start us, length us, event | category | flops | bytes accessed | tf_op | source)
XLA Modules:
  0.0 116.8 jit_solution(6261359013212595276)
XLA Ops:
  0.6 0.8 convert_reduce_fusion.1
  2.1 0.9 fusion.1
  2.9 0.0 copy-start.1
  2.9 0.0 copy-start.2
  3.0 11.5 %conditional.12 = (bf16[240,256]{1,0:T(8,128)(2,1)}, bf16[14,256]{1,0:T(8,128)(2,1)S(1)}, bf16[224,256]{1,0:T(8,128)(2,1)S(1)}, s32[1,3584]{1,0:T(1,128)S(1)}) conditional(s32[]{:T(128)} %bitcast.1, bf16[240,256]{1,0:T(8,128)(2,1)S(1)} %fusion.1, bf16[240,256]{1,0:T(8,128)(2,1)S(1)} %fusion.1, ...), branch_computations={%region_0.1_spmd, %region_1.2_spmd, %region_2.3_spmd, %region_3.4_... | conditional | flops 3584 | bytes 778312
  3.0 6.3 %collective-permute-start.21 = (bf16[240,256]{1,0:T(8,128)(2,1)S(1)}, bf16[240,256]{1,0:T(8,128)(2,1)}, u32[]{:S(2)}, u32[]{:S(2)}) collective-permute-start(bf16[240,256]{1,0:T(8,128)(2,1)S(1)} %param.6), channel_id=1, source_target_pairs={{0,112},{16,96},{32,80},{48,64},{64,48},{80,32},{96,16},{112,0},{1... | collective-permute-start | bytes 368648 | tf_op jit(solution)/shard_map/cond/branch_6_fun/ppermute | solution.py:200
  9.3 3.5 %collective-permute-done.21 = bf16[240,256]{1,0:T(8,128)(2,1)} collective-permute-done((bf16[240,256]{1,0:T(8,128)(2,1)S(1)}, bf16[240,256]{1,0:T(8,128)(2,1)}, u32[]{:S(2)}, u32[]{:S(2)}) %collective-permute-start.21) | collective-permute-done | bytes 122912 | tf_op jit(solution)/shard_map/cond/branch_6_fun/ppermute | solution.py:200
  12.8 0.7 convert_bitcast_fusion.6
  13.5 0.9 slice.126
  14.4 0.0 copy-done.1
  14.4 0.0 copy-done.2
  14.5 0.2 broadcast_in_dim.25
  14.7 1.4 %pad_maximum_fusion = bf16[16,224,256]{2,1,0:T(8,128)(2,1)} fusion(bf16[1,224,256]{2,1,0:T(8,128)(2,1)S(1)} %get-tuple-element.115, bf16[15,224,256]{2,1,0:T(8,128)(2,1)S(1)} %broadcast_in_dim.25), kind=kLoop, calls=%fused_computation.16 | loop fusion | flops 917504 | bytes 3670016 | tf_op jit(solution)/shard_map/concatenate | solution.py:215
  16.1 0.0 copy-start.3
  16.1 6.1 %all-to-all-start = ((bf16[16,224,256]{2,1,0:T(8,128)(2,1)}), bf16[16,224,256]{2,1,0:T(8,128)(2,1)S(1)}, u32[]{:S(2)}, u32[]{:S(2)}) async-start(bf16[16,224,256]{2,1,0:T(8,128)(2,1)} %pad_maximum_fusion), calls=%async_computation | async-start | bytes 3670016 | tf_op jit(solution)/shard_map/all_to_all | solution.py:218
  22.2 0.0 copy-done.3
  22.2 0.6 broadcast_select_fusion.docs
  22.8 23.2 %all-to-all-done = bf16[16,224,256]{2,1,0:T(8,128)(2,1)S(1)} async-done(((bf16[16,224,256]{2,1,0:T(8,128)(2,1)}), bf16[16,224,256]{2,1,0:T(8,128)(2,1)S(1)}, u32[]{:S(2)}, u32[]{:S(2)}) %all-to-all-start) | async-done | bytes 1835040 | tf_op jit(solution)/shard_map/all_to_all | solution.py:218
  46.0 0.0 copy-start
  46.0 1.3 %copy-done = bf16[16,224,256]{2,1,0:T(8,128)(2,1)} copy-done((bf16[16,224,256]{2,1,0:T(8,128)(2,1)}, bf16[16,224,256]{2,1,0:T(8,128)(2,1)S(1)}, u32[]{:S(2)}) %copy-start) | copy-done | bytes 1835032
  47.3 9.5 %attention.1 = (bf16[224,1024]{1,0:T(8,128)(2,1)}, bf16[224,1024]{1,0:T(8,128)(2,1)}, bf16[3584,256]{1,0:T(8,128)(2,1)}) custom-call(s32[1]{0:T(128)} %bitcast.device, s32[1,3584]{1,0:T(1,128)} %broadcast_select_fusion.docs, bf16[224,1024]{1,0:T(8,128)(2,1)} %bitcast.102, bf16[224,1024]{1,0:T(8,128)(2,1)} %bitcast.103, bf16[3584,256]{1,0:T(8,128)(2,1)} %bitcast.81), custom_call_target="tpu_custom_call" | custom-call | flops 4932501504 | bytes 6291456 | tf_op jit(solution)/shard_map/attention/pallas_call | solution.py:162
  56.8 47.8 %all_to_all.10 = bf16[16,224,256]{2,1,0:T(8,128)(2,1)S(1)} all-to-all(bf16[16,224,256]{2,1,0:T(8,128)(2,1)} %bitcast.82), channel_id=1, replica_groups=mesh['dp'=16,'ctx'=16] {'ctx'}, dimensions={0} | all-to-all | bytes 3670016 | tf_op jit(solution)/shard_map/all_to_all | solution.py:225
  104.5 10.4 %conditional.13 = (bf16[224,256]{1,0:T(8,128)(2,1)}) conditional(s32[]{:T(128)} %bitcast.1, bf16[224,256]{1,0:T(8,128)(2,1)S(1)} %slice_bitcast_fusion, bf16[224,256]{1,0:T(8,128)(2,1)S(1)} %slice_bitcast_fusion, bf16[224,256]{1,0:T(8,128)(2,1)S(1)} %slice_bitcast_fusion, ...), branch_computations={%region_16.17_spmd, %region_17.18_spmd, %region_18.19_spmd, %regio... | conditional | bytes 458800
  104.6 6.8 %collective-permute-start.6 = (bf16[224,256]{1,0:T(8,128)(2,1)S(1)}, bf16[224,256]{1,0:T(8,128)(2,1)}, u32[]{:S(2)}, u32[]{:S(2)}) collective-permute-start(bf16[224,256]{1,0:T(8,128)(2,1)S(1)} %param.21), channel_id=1, source_target_pairs={{0,112},{16,96},{32,80},{48,64},{64,48},{80,32},{96,16},{112,0},{1... | collective-permute-start | bytes 344072 | tf_op jit(solution)/shard_map/cond/branch_6_fun/ppermute | solution.py:200
  111.3 3.6 %collective-permute-done.6 = bf16[224,256]{1,0:T(8,128)(2,1)} collective-permute-done((bf16[224,256]{1,0:T(8,128)(2,1)S(1)}, bf16[224,256]{1,0:T(8,128)(2,1)}, u32[]{:S(2)}, u32[]{:S(2)}) %collective-permute-start.6) | collective-permute-done | bytes 114720 | tf_op jit(solution)/shard_map/cond/branch_6_fun/ppermute | solution.py:200
  115.0 0.2 convert_reduce_fusion
  115.2 0.9 select_convert_fusion
  116.2 0.6 slice_bitcast_fusion.1
  (4 shorter events, 0.1 us)
Async XLA Ops:
  2.9 11.5 %copy-start.1 = (bf16[1,224,128]{2,1,0:T(8,128)(2,1)S(1)}, bf16[1,224,128]{2,1,0:T(8,128)(2,1)}, u32[]{:S(2)}) copy-start(bf16[1,224,128]{2,1,0:T(8,128)(2,1)} %param.38) | copy-start | bytes 172036
  2.9 11.5 %copy-start.2 = (bf16[1,224,128]{2,1,0:T(8,128)(2,1)S(1)}, bf16[1,224,128]{2,1,0:T(8,128)(2,1)}, u32[]{:S(2)}) copy-start(bf16[1,224,128]{2,1,0:T(8,128)(2,1)} %param.37) | copy-start | bytes 172036
  3.0 9.8 %collective-permute-start.21 = (bf16[240,256]{1,0:T(8,128)(2,1)S(1)}, bf16[240,256]{1,0:T(8,128)(2,1)}, u32[]{:S(2)}, u32[]{:S(2)}) collective-permute-start(bf16[240,256]{1,0:T(8,128)(2,1)S(1)} %param.6), channel_id=1, source_target_pairs={{0,112},{16,96},{32,80},{48,64},{64,48},{80,32},{96,16},{112,0},{1... | collective-permute-start | bytes 368648 | tf_op jit(solution)/shard_map/cond/branch_6_fun/ppermute | solution.py:200
  16.1 6.1 %copy-start.3 = (s32[1,3584]{1,0:T(1,128)S(1)}, s32[1,3584]{1,0:T(1,128)}, u32[]{:S(2)}) copy-start(s32[1,3584]{1,0:T(1,128)} %param.40) | copy-start | bytes 43012
  16.1 29.9 %all-to-all-start = ((bf16[16,224,256]{2,1,0:T(8,128)(2,1)}), bf16[16,224,256]{2,1,0:T(8,128)(2,1)S(1)}, u32[]{:S(2)}, u32[]{:S(2)}) async-start(bf16[16,224,256]{2,1,0:T(8,128)(2,1)} %pad_maximum_fusion), calls=%async_computation | async-start | bytes 3670016 | tf_op jit(solution)/shard_map/all_to_all | solution.py:218
  46.0 1.3 %copy-start = (bf16[16,224,256]{2,1,0:T(8,128)(2,1)}, bf16[16,224,256]{2,1,0:T(8,128)(2,1)S(1)}, u32[]{:S(2)}) copy-start(bf16[16,224,256]{2,1,0:T(8,128)(2,1)S(1)} %all-to-all-done) | copy-start | bytes 5505028
  104.6 10.4 %collective-permute-start.6 = (bf16[224,256]{1,0:T(8,128)(2,1)S(1)}, bf16[224,256]{1,0:T(8,128)(2,1)}, u32[]{:S(2)}, u32[]{:S(2)}) collective-permute-start(bf16[224,256]{1,0:T(8,128)(2,1)S(1)} %param.21), channel_id=1, source_target_pairs={{0,112},{16,96},{32,80},{48,64},{64,48},{80,32},{96,16},{112,0},{1... | collective-permute-start | bytes 344072 | tf_op jit(solution)/shard_map/cond/branch_6_fun/ppermute | solution.py:200
where the time goes:
time: 119 us; the launch traced here: 117 us
  blocking collectives  47.8 us (40%)
  waiting for transfers between devices  30.4 us (26%)
  starting transfers between devices  19.1 us (16%)
  Pallas kernels  9.47 us (8%)
  other arithmetic  5.6 us (5%)
  local copies, waits for them, and re-layouts  3.05 us (3%)
  between operations  1.36 us (1%)
    all_to_all x1, blocking collectives, on_device(): lax.all_to_all(terms.reshape(ctx_size, span, 2 * width), 'ctx', 0, 0)  47.8 us
    all_to_all x1, waiting for transfers between devices, on_device(): lax.all_to_all(sending, 'ctx', 0, 0).reshape(ctx_size * span, 2 * width)  23.2 us
    ppermute x2, starting transfers between devices, turn(): lax.ppermute(v, 'dp', [(i, i ^ mask) for i in range(dp_size)])  13 us
    pallas_call x1, Pallas kernels, attention(): pl.pallas_call(kernel, out_shape=(jax.ShapeDtypeStruct((span, features),...  9.47 us
    ppermute x2, waiting for transfers between devices, turn(): lax.ppermute(v, 'dp', [(i, i ^ mask) for i in range(dp_size)])  7.16 us
    all_to_all x1, starting transfers between devices, on_device(): lax.all_to_all(sending, 'ctx', 0, 0).reshape(ctx_size * span, 2 * width)  6.08 us
  transfers between devices with their start and end apart: 3, of which 3 were waited for; matrix products, arithmetic and copies ran while one was open for 1% of the time, Pallas kernels for 0%

commit v1 on v0

v1 whole, which is shorter than its diff:
```python
import functools
import math

import jax
import jax.numpy as jnp
from jax import lax
from jax.experimental import pallas as pl
from jax.experimental.pallas import tpu as pltpu
from jax.sharding import PartitionSpec as P

TILE = 512
LANES = 256
BF16, F32, I32 = jnp.bfloat16, jnp.float32, jnp.int32


def dot(a, b, ca, cb):
    return lax.dot_general(a, b, (((ca,), (cb,)), ((), ())), preferred_element_type=F32)


def head_copies(wide, stacked, sem, to_stacked):
    span, width = wide.shape[0], stacked.shape[1]
    made = []
    for h in range(wide.shape[1] // width):
        a = wide.at[:, h * width : (h + 1) * width]
        b = stacked.at[h * span : (h + 1) * span, :]
        a, b = (a, b) if to_stacked else (b, a)
        made.append(pltpu.make_async_copy(a, b, sem.at[h]))
    return made


def begin(copies):
    for c in copies:
        c.start()


def finish(copies):
    for c in copies:
        c.wait()


def kept_at(t):
    return pl.ds(pl.multiple_of(t * TILE, TILE), TILE)


def softmax_kernel(
    span, scale,
    device, docs, query, keys_in,
    probs, total, bounds,
    q_rows, keys, scores, weights, top, low, in_sem, key_sem, out_sem,
):
    rows, width = q_rows.shape
    key_count = keys.shape[0]
    heads = rows // span
    chunks = [slice(r, r + LANES) for r in range(0, rows, LANES)]
    factor = scale * math.log2(math.e)
    offset = device[0] * span

    arriving = head_copies(query, q_rows, in_sem, True)
    arriving.append(pltpu.make_async_copy(keys_in, keys, key_sem))
    begin(arriving)

    names = docs[...]
    row = pltpu.roll(names, lax.rem(key_count - offset, key_count), 1)[:, 0:span]
    start = jnp.zeros((1, span), I32)
    for d in range(1, 8):
        before = jnp.sum((names < d).astype(I32), axis=1, keepdims=True)
        start = jnp.where(row == d, before, start)
    place = offset + lax.broadcasted_iota(I32, (1, span), 1)
    for h in range(heads):
        low[0:1, h * span : (h + 1) * span] = start
        low[1:2, h * span : (h + 1) * span] = place
    low_first, low_last = jnp.min(start), jnp.max(start)
    end = offset + span
    count = lax.div(end - low_first + TILE - 1, TILE)
    base = jnp.maximum(end - count * TILE, 0)
    clear = jnp.minimum(lax.div(jnp.maximum(low_last - base, 0) + TILE - 1, TILE), count)
    full = jnp.minimum(jnp.maximum(lax.div(offset + 1 - base, TILE), clear), count)
    bounds[0] = base
    bounds[1] = count

    top[...] = jnp.full(top.shape, -jnp.inf, F32)
    total[...] = jnp.zeros(total.shape, F32)
    finish(arriving)

    def score_tile(t, masked):
        key = keys[pl.ds(pl.multiple_of(base + t * TILE, 32), TILE), :]
        for c in chunks:
            s = dot(key, q_rows[c, :], 1, 1)
            if masked:
                at = base + t * TILE + lax.broadcasted_iota(I32, (TILE, LANES), 0)
                ok = (at >= low[0:1, c]) & (at <= low[1:2, c])
                s = jnp.where(ok, s, -jnp.inf)
            scores[kept_at(t), c] = s
            top[:, c] = jnp.maximum(top[:, c], jnp.max(s.reshape(TILE // 8, 8, LANES), axis=0))

    @pl.loop(0, clear)
    def _(t):
        score_tile(t, True)

    @pl.loop(clear, full)
    def _(t):
        score_tile(t, False)

    @pl.loop(full, count)
    def _(t):
        score_tile(t, True)

    peak = jnp.max(top[...], axis=0, keepdims=True) * factor
    top[...] = jnp.broadcast_to(peak, top.shape)

    def leaving(t):
        return pltpu.make_async_copy(weights.at[kept_at(t)], probs.at[kept_at(t)], out_sem.at[t])

    @pl.loop(0, count)
    def _(t):
        for c in chunks:
            p = jnp.exp2(scores[kept_at(t), c] * factor - top[0:1, c])
            total[:, c] += jnp.sum(p.reshape(TILE // 8, 8, LANES), axis=0)
            weights[kept_at(t), c] = p.astype(BF16)
        leaving(t).start()

    @pl.loop(0, count)
    def _(t):
        leaving(t).wait()


def output_kernel(
    bounds, total, grad, values_in, probs,
    out, g_cols, delta, dvalues_out,
    g_rows, o_rows, values, dvalues, weights, out_t, in_sem, value_sem, prob_sem, out_sem,
):
    rows, width = g_rows.shape
    base, count = bounds[0], bounds[1]

    def arriving(t):
        return pltpu.make_async_copy(probs.at[kept_at(t)], weights.at[kept_at(t)], prob_sem.at[t])

    values_copy = pltpu.make_async_copy(values_in, values, value_sem)
    values_copy.start()

    @pl.loop(0, count)
    def _(t):
        arriving(t).start()

    grad_copies = head_copies(grad, g_rows, in_sem, True)
    begin(grad_copies)
    out_t[...] = jnp.zeros(out_t.shape, F32)
    dvalues[...] = jnp.zeros(dvalues.shape, BF16)
    inverse = 1.0 / jnp.sum(total[...], axis=0, keepdims=True)
    finish(grad_copies)
    for r in range(0, rows, 128):
        c = slice(r, r + 128)
        g_cols[:, c] = (g_rows[c, :].T.astype(F32) * inverse[:, c]).astype(BF16)
    values_copy.wait()

    def keys_at(t):
        return pl.ds(pl.multiple_of(base + t * TILE, 32), TILE)

    @pl.loop(0, count)
    def _(t):
        arriving(t).wait()
        value_t = values[keys_at(t), :].T
        out_t[...] += dot(value_t, weights[kept_at(t), :], 1, 0)
        dvalues[keys_at(t), :] = dot(weights[kept_at(t), :], g_cols[...], 1, 1).astype(BF16)

    leaving = [pltpu.make_async_copy(dvalues, dvalues_out, value_sem)]
    begin(leaving)
    for r in range(0, rows, 128):
        c = slice(r, r + 128)
        o = out_t[:, c] * inverse[:, c]
        delta[0:1, c] = jnp.sum(g_cols[:, c].astype(F32) * o, axis=0, keepdims=True)
        o_rows[c, :] = o.T.astype(BF16)
    out_copies = head_copies(out, o_rows, out_sem, False)
    begin(out_copies)
    finish(leaving + out_copies)


def gradient_kernel(
    scale,
    bounds, g_cols, delta, query, keys_in, values_in, probs,
    dquery, dkeys_out,
    q_rows, keys, values, dkeys, weights, dscores, dq_t, in_sem, pair_sem, prob_sem, out_sem,
):
    rows, width = q_rows.shape
    chunks = [slice(r, r + LANES) for r in range(0, rows, LANES)]
    base, count = bounds[0], bounds[1]

    def arriving(t):
        return pltpu.make_async_copy(probs.at[kept_at(t)], weights.at[kept_at(t)], prob_sem.at[t])

    pair_copies = [
        pltpu.make_async_copy(values_in, values, pair_sem.at[0]),
        pltpu.make_async_copy(keys_in, keys, pair_sem.at[1]),
    ]
    begin(pair_copies)

    @pl.loop(0, count)
    def _(t):
        arriving(t).start()

    query_copies = head_copies(query, q_rows, in_sem, True)
    begin(query_copies)
    dq_t[...] = jnp.zeros(dq_t.shape, F32)
    dkeys[...] = jnp.zeros(dkeys.shape, BF16)
    finish(pair_copies + query_copies)

    @pl.loop(0, count)
    def _(t):
        at = pl.ds(pl.multiple_of(base + t * TILE, 32), TILE)
        kept = kept_at(t)
        arriving(t).wait()
        value = values[at, :]
        for c in chunks:
            dp = dot(value, g_cols[:, c], 1, 0)
            dscores[:, c] = weights[kept, c] * (dp - delta[0:1, c]).astype(BF16)
        dk = dot(dscores[...], q_rows[...], 1, 0)
        dkeys[at, :] = (dk * scale).astype(BF16)
        dq_t[...] += dot(keys[at, :].T, dscores[...], 1, 0)

    leaving = [pltpu.make_async_copy(dkeys, dkeys_out, pair_sem.at[0])]
    begin(leaving)
    for r in range(0, rows, 128):
        q_rows[r : r + 128, :] = (dq_t[:, r : r + 128].T * scale).astype(BF16)
    out_copies = head_copies(dquery, q_rows, out_sem, False)
    begin(out_copies)
    finish(leaving + out_copies)


VMEM = pl.BlockSpec(memory_space=pltpu.VMEM)
SMEM = pl.BlockSpec(memory_space=pltpu.SMEM)
HBM = pl.BlockSpec(memory_space=pl.ANY)


def call(kernel, name, products, sizes, in_specs, outs, scratch):
    rows, keys, width = sizes
    return pl.pallas_call(
        kernel,
        out_shape=tuple(jax.ShapeDtypeStruct(shape, dtype) for shape, dtype, _ in outs),
        in_specs=in_specs,
        out_specs=tuple(spec for _, _, spec in outs),
        scratch_shapes=scratch,
        compiler_params=pltpu.CompilerParams(vmem_limit_bytes=50 * 1024 * 1024),
        cost_estimate=pl.CostEstimate(
            flops=products * 3 * rows * keys * width, bytes_accessed=20 << 20, transcendentals=0
        ),
        name=name,
    )


def local(device, docs, query, grad, all_keys, all_values, exchange):
    span, features = query.shape
    keys, width = all_keys.shape
    heads = features // width
    rows, most = heads * span, keys // TILE
    sizes = (rows, keys, width)
    scale = 1.0 / math.sqrt(width)
    dma = pltpu.SemaphoreType.DMA
    probs, total, bounds = call(
        functools.partial(softmax_kernel, span, scale), "softmax", 1, sizes,
        [SMEM, VMEM, HBM, HBM],
        [((keys, rows), BF16, HBM), ((8, rows), F32, VMEM), ((2,), I32, SMEM)],
        [
            pltpu.VMEM((rows, width), BF16), pltpu.VMEM((keys, width), BF16),
            pltpu.VMEM((keys, rows), F32), pltpu.VMEM((keys, rows), BF16),
            pltpu.VMEM((8, rows), F32), pltpu.VMEM((8, rows), I32),
            dma((heads,)), dma, dma((most,)),
        ],
    )(device, docs, query, all_keys)
    out, g_cols, delta, dvalues = call(
        output_kernel, "output", 2, sizes,
        [SMEM, VMEM, HBM, HBM, HBM],
        [
            ((span, features), BF16, HBM), ((width, rows), BF16, VMEM),
            ((8, rows), F32, VMEM), ((keys, width), BF16, HBM),
        ],
        [
            pltpu.VMEM((rows, width), BF16), pltpu.VMEM((rows, width), BF16),
            pltpu.VMEM((keys, width), BF16), pltpu.VMEM((keys, width), BF16),
            pltpu.VMEM((keys, rows), BF16), pltpu.VMEM((width, rows), F32),
            dma((heads,)), dma, dma((most,)), dma((heads,)),
        ],
    )(bounds, total, grad, all_values, probs)
    dvalue_terms = exchange(dvalues)
    dquery, dkeys = call(
        functools.partial(gradient_kernel, scale), "gradient", 3, sizes,
        [SMEM, VMEM, VMEM, HBM, HBM, HBM, HBM],
        [((span, features), BF16, HBM), ((keys, width), BF16, HBM)],
        [
            pltpu.VMEM((rows, width), BF16), pltpu.VMEM((keys, width), BF16),
            pltpu.VMEM((keys, width), BF16), pltpu.VMEM((keys, width), BF16),
            pltpu.VMEM((keys, rows), BF16), pltpu.VMEM((TILE, rows), BF16),
            pltpu.VMEM((width, rows), F32),
            dma((heads,)), dma((2,)), dma((most,)), dma((heads,)),
        ],
    )(bounds, g_cols, delta, query, all_keys, all_values, probs)
    return out, dquery, dkeys, dvalue_terms


def across(block, matching, dp_size):
    def turn(mask):
        return lambda v: lax.ppermute(v, "dp", [(i, i ^ mask) for i in range(dp_size)])

    return lax.switch(matching[0] - 1, [turn(mask) for mask in range(1, dp_size)], block)


def on_device(query_rows, key_rows, value_rows, out_grad, doc_ids, matching):
    ctx_size, dp_size = lax.axis_size("ctx"), lax.axis_size("dp")
    me = lax.axis_index("ctx")
    span, width = key_rows.shape[1:]
    keys = ctx_size * span
    is_last = me == ctx_size - 1
    stored = jnp.concatenate([key_rows[0], value_rows[0]], axis=1)
    names = doc_ids.astype(BF16).reshape(-1, 2 * width)
    names = jnp.pad(names, ((0, -names.shape[0] % 16), (0, 0)))
    arrived = across(jnp.concatenate([stored, names], axis=0), matching, dp_size)

    def exchange(blocks):
        return lax.all_to_all(blocks, "ctx", 0, 0)

    def exchange_rows(terms):
        return exchange(terms.reshape(ctx_size, span, width))

    def gather(own, part):
        last = jnp.where(is_last, own, arrived[:span, part])
        which = lax.broadcasted_iota(I32, (ctx_size, 1, 1), 0) == ctx_size - 1
        return exchange(jnp.where(which, last[None], own[None])).reshape(keys, width)

    all_keys = gather(key_rows[0], slice(0, width))
    all_values = gather(value_rows[0], slice(width, 2 * width))
    doc_rows = doc_ids.shape[1] // (2 * width)
    far = arrived[span : span + doc_rows].reshape(1, -1).astype(I32)
    docs = jnp.where(is_last, far, doc_ids)
    out, dquery, dkeys, dvalue_terms = local(
        me.astype(I32)[None], docs, query_rows[0], out_grad[0], all_keys, all_values, exchange_rows
    )
    dkey_terms = exchange_rows(dkeys)
    both = (dkey_terms, dvalue_terms)
    tail = jnp.concatenate([terms[ctx_size - 1] for terms in both], axis=1)
    back = across(tail, matching, dp_size)

    def final(terms, part):
        own = jnp.sum(terms[: ctx_size - 1].astype(F32), axis=0) + back[:, part].astype(F32)
        return jnp.where(is_last, terms[ctx_size - 1].astype(F32), own).astype(BF16)[None]

    return (
        out[None],
        dquery[None],
        final(dkey_terms, slice(0, width)),
        final(dvalue_terms, slice(width, 2 * width)),
    )


def solution(mesh):
    rows = P("dp", "ctx", None)
    return jax.shard_map(
        on_device,
        mesh=mesh,
        in_specs=(rows, rows, rows, rows, P("dp", None), P()),
        out_specs=(rows, rows, rows, rows),
        check_vma=False,
    )
```

time: 119 us -> 119 us (level); the launches traced: 117 us -> 119 us
  blocking collectives: 47.8 us -> 0 us
  waiting for transfers between devices: 30.4 us -> 56.1 us
  starting transfers between devices: 19.1 us -> 37.3 us
  Pallas kernels: 9.47 us -> 14.3 us
  other arithmetic: 5.6 us -> 8.55 us
  local copies, waits for them, and re-layouts: 3.05 us -> 0.87 us
    all_to_all x1 -> x0, blocking collectives: 47.8 us -> none  [on_device(): lax.all_to_all(terms.reshape(ctx_size, span, 2 * width), 'ctx', 0, 0)]
    all_to_all x1 -> x4, waiting for transfers between devices: 23.2 us -> 44.7 us  [exchange(): return lax.all_to_all(blocks, 'ctx', 0, 0)]
    all_to_all x1 -> x4, starting transfers between devices: 6.08 us -> 24.4 us  [exchange(): return lax.all_to_all(blocks, 'ctx', 0, 0)]
    pallas_call x1 -> x3, Pallas kernels: 9.47 us -> 14.3 us  [the longest x1 5.13 us: local(): call(functools.partial(gradient_kernel, scale), 'gradient', 3, sizes, [SM...]
    ppermute x2, waiting for transfers between devices: 7.16 us -> 11.4 us  [turn(): lax.ppermute(v, 'dp', [(i, i ^ mask) for i in range(dp_size)])]
    select_n x0 -> x2, other arithmetic: none -> 3.22 us  [the longest x1 2.31 us: gather(): jnp.where(which, last[None], own[None])]
    broadcast_in_dim x0 -> x1, other arithmetic: none -> 1.56 us  [final(): jnp.where(is_last, terms[ctx_size - 1].astype(F32), own).astype(BF16)[None]]
    concatenate x2 -> x1, other arithmetic: 1.48 us -> 0.01 us  [on_device(): tail = jnp.concatenate([terms[ctx_size - 1] for terms in both], axis=1)]
  transfers between devices with their start and end apart: 3 -> 6, of which waited for: 3 -> 6; matrix products, arithmetic and copies ran while one was open for 1% -> 1% of each run, Pallas kernels for 0% -> 8%
where the time goes in v1:
time: 119 us
  waiting for transfers between devices  56.1 us (47%)
  starting transfers between devices  37.3 us (31%)
  Pallas kernels  14.3 us (12%)
  other arithmetic  8.55 us (7%)
  between operations  1.38 us (1%)
    all_to_all x4, waiting for transfers between devices, exchange(): return lax.all_to_all(blocks, 'ctx', 0, 0)  44.7 us
    all_to_all x4, starting transfers between devices, exchange(): return lax.all_to_all(blocks, 'ctx', 0, 0)  24.4 us
    ppermute x2, starting transfers between devices, turn(): lax.ppermute(v, 'dp', [(i, i ^ mask) for i in range(dp_size)])  13 us
    ppermute x2, waiting for transfers between devices, turn(): lax.ppermute(v, 'dp', [(i, i ^ mask) for i in range(dp_size)])  11.4 us
    pallas_call x1, Pallas kernels, local(): call(functools.partial(gradient_kernel, scale), 'gradient', 3, sizes, [SM...  5.13 us
    pallas_call x1, Pallas kernels, local(): call(output_kernel, 'output', 2, sizes, [SMEM, VMEM, HBM, HBM, HBM], [((s...  4.66 us
    pallas_call x1, Pallas kernels, local(): call(functools.partial(softmax_kernel, span, scale), 'softmax', 1, sizes,...  4.55 us
  transfers between devices with their start and end apart: 6, of which 6 were waited for; matrix products, arithmetic and copies ran while one was open for 1% of the time, Pallas kernels for 8%

profile of v1, /device:TPU:2, one launch (start us, length us, event | category | flops | bytes accessed | tf_op | source)
XLA Modules:
  0.0 118.7 jit_solution(493624289869759133)
XLA Ops:
  0.6 0.8 convert_reduce_fusion.2
  2.1 0.9 fusion.1
  2.9 13.6 %conditional.2 = (bf16[240,256]{1,0:T(8,128)(2,1)}) conditional(s32[]{:T(128)} %bitcast.1, bf16[240,256]{1,0:T(8,128)(2,1)S(1)} %fusion.1, bf16[240,256]{1,0:T(8,128)(2,1)S(1)} %fusion.1, bf16[240,256]{1,0:T(8,128)(2,1)S(1)} %fusion.1, bf16[240,256]{1,0:T(8,128)(2,1)S(1)} %fusion.1, ...), branch_computations={%region_0.1_spmd, %region_1.2_spmd, %region_2.3_spmd, %region_3.4_... | conditional | bytes 491568 | solution.py:303
  3.0 7.5 %collective-permute-start.14 = (bf16[240,256]{1,0:T(8,128)(2,1)S(1)}, bf16[240,256]{1,0:T(8,128)(2,1)}, u32[]{:S(2)}, u32[]{:S(2)}) collective-permute-start(bf16[240,256]{1,0:T(8,128)(2,1)S(1)} %param.14), channel_id=1, source_target_pairs={{0,240},{16,224},{32,208},{48,192},{64,176},{80,160},{96,144},{112... | collective-permute-start | bytes 368648 | tf_op jit(solution)/shard_map/cond/branch_14_fun/ppermute | solution.py:301
  10.5 6.1 %collective-permute-done.14 = bf16[240,256]{1,0:T(8,128)(2,1)} collective-permute-done((bf16[240,256]{1,0:T(8,128)(2,1)S(1)}, bf16[240,256]{1,0:T(8,128)(2,1)}, u32[]{:S(2)}, u32[]{:S(2)}) %collective-permute-start.14) | collective-permute-done | bytes 122912 | tf_op jit(solution)/shard_map/cond/branch_14_fun/ppermute | solution.py:301
  16.6 0.9 slice_select_fusion
  17.5 2.3 %broadcast_select_fusion = (bf16[16,224,128]{2,1,0:T(8,128)(2,1)}, bf16[16,224,128]{2,1,0:T(8,128)(2,1)}) fusion(pred[16]{0:T(512)(128)(4,1)S(1)} %iota_compare_fusion.1, bf16[224,128]{1,0:T(8,128)(2,1)} %bitcast.39, bf16[224,128]{1,0:T(8,128)(2,1)S(1)} %get-tuple-element.84, bf16[224,128]{1,0:T(8,128)(2,1)} %bitcast.41, ...), kind=kLoop, calls=%fused_computation.2 | loop fusion | flops 917504 | bytes 2064400 | tf_op jit(solution)/shard_map/jit(_where)/select_n | solution.py:326
  19.8 0.0 copy-start.2
  19.8 0.0 copy-start.1
  19.8 6.1 %all-to-all-start = ((bf16[16,224,128]{2,1,0:T(8,128)(2,1)}), bf16[16,224,128]{2,1,0:T(8,128)(2,1)S(1)}, u32[]{:S(2)}, u32[]{:S(2)}) async-start(bf16[16,224,128]{2,1,0:T(8,128)(2,1)} %get-tuple-element.89), calls=%async_computation | async-start | bytes 1835008 | tf_op jit(solution)/shard_map/all_to_all | solution.py:318
  25.9 0.7 convert_bitcast_fusion
  26.6 13.2 %all-to-all-done = bf16[16,224,128]{2,1,0:T(8,128)(2,1)S(1)} async-done(((bf16[16,224,128]{2,1,0:T(8,128)(2,1)}), bf16[16,224,128]{2,1,0:T(8,128)(2,1)S(1)}, u32[]{:S(2)}, u32[]{:S(2)}) %all-to-all-start) | async-done | bytes 917536 | tf_op jit(solution)/shard_map/all_to_all | solution.py:318
  39.8 4.7 %all-to-all-start.1 = ((bf16[16,224,128]{2,1,0:T(8,128)(2,1)}), bf16[16,224,128]{2,1,0:T(8,128)(2,1)S(1)}, u32[]{:S(2)}, u32[]{:S(2)}) async-start(bf16[16,224,128]{2,1,0:T(8,128)(2,1)} %get-tuple-element.88), calls=%async_computation.1 | async-start | bytes 1835008 | tf_op jit(solution)/shard_map/all_to_all | solution.py:318
  44.6 0.0 copy-done.2
  44.6 0.0 copy-done.1
  44.6 0.0 copy-start
  44.6 4.6 %softmax.1 = (bf16[3584,1792]{1,0:T(8,128)(2,1)}, f32[8,1792]{1,0:T(8,128)S(1)}, s32[2]{0:T(128)S(1)}) custom-call(s32[1]{0:T(128)} %bitcast.device, s32[1,3584]{1,0:T(1,128)S(1)} %broadcast_select_fusion.2.docs, bf16[224,1024]{1,0:T(8,128)(2,1)S(1)} %bitcast.36, bf16[3584,128]{1,0:T(8,128)(2,1)S(1)} %bitcast.31), custom_call_target="tpu_custom_call" | custom-call | flops 2466250752 | bytes 20971520 | tf_op jit(solution)/shard_map/softmax/pallas_call | solution.py:258
  49.2 9.4 %all-to-all-done.1 = bf16[16,224,128]{2,1,0:T(8,128)(2,1)S(1)} async-done(((bf16[16,224,128]{2,1,0:T(8,128)(2,1)}), bf16[16,224,128]{2,1,0:T(8,128)(2,1)S(1)}, u32[]{:S(2)}, u32[]{:S(2)}) %all-to-all-start.1) | async-done | bytes 917536 | tf_op jit(solution)/shard_map/all_to_all | solution.py:318
  58.5 0.0 copy-done
  58.5 4.7 %output.1 = (bf16[224,1024]{1,0:T(8,128)(2,1)}, bf16[128,1792]{1,0:T(8,128)(2,1)S(1)}, f32[8,1792]{1,0:T(8,128)S(1)}, bf16[3584,128]{1,0:T(8,128)(2,1)}) custom-call(s32[2]{0:T(128)S(1)} %get-tuple-element.75.bounds, f32[8,1792]{1,0:T(8,128)S(1)} %get-tuple-element.76.total, bf16[224,1024]{1,0:T(8,128)(2,1)S(1)} %bitcast.35, bf16[3584,128]{1,0:T(8,128)(2,1)S(1)} %bitcast.33, ...), custom_call_target="tpu_custom_call" | custom-call | flops 4932501504 | bytes 20971520 | tf_op jit(solution)/shard_map/output/pallas_call | solution.py:269
  63.2 8.8 %all-to-all-start.3 = ((bf16[16,224,128]{2,1,0:T(8,128)(2,1)}), bf16[16,224,128]{2,1,0:T(8,128)(2,1)}, u32[]{:S(2)}, u32[]{:S(2)}) async-start(bf16[16,224,128]{2,1,0:T(8,128)(2,1)} %bitcast.12), calls=%async_computation.3 | async-start | bytes 1835008 | tf_op jit(solution)/shard_map/all_to_all | solution.py:318
  72.0 5.1 %gradient.1 = (bf16[224,1024]{1,0:T(8,128)(2,1)}, bf16[3584,128]{1,0:T(8,128)(2,1)}) custom-call(s32[2]{0:T(128)S(1)} %get-tuple-element.75.bounds, bf16[128,1792]{1,0:T(8,128)(2,1)S(1)} %get-tuple-element.79.g_cols, f32[8,1792]{1,0:T(8,128)S(1)} %get-tuple-element.80.delta, bf16[224,1024]{1,0:T(8,128)(2,1)S(1)} %bitcast.37, bf16[3584,128]{1,0:T(8,128)(2,1)S(1)} %bitcast.32, ...), custom_call_target="tpu_custom_call" | custom-call | flops 7398752256 | bytes 20971520 | tf_op jit(solution)/shard_map/gradient/pallas_call | solution.py:284
  77.2 8.9 %all-to-all-done.3 = bf16[16,224,128]{2,1,0:T(8,128)(2,1)} async-done(((bf16[16,224,128]{2,1,0:T(8,128)(2,1)}), bf16[16,224,128]{2,1,0:T(8,128)(2,1)}, u32[]{:S(2)}, u32[]{:S(2)}) %all-to-all-start.3) | async-done | bytes 917536 | tf_op jit(solution)/shard_map/all_to_all | solution.py:318
  86.1 4.7 %all-to-all-start.2 = ((bf16[16,224,128]{2,1,0:T(8,128)(2,1)}), bf16[16,224,128]{2,1,0:T(8,128)(2,1)S(1)}, u32[]{:S(2)}, u32[]{:S(2)}) async-start(bf16[16,224,128]{2,1,0:T(8,128)(2,1)} %bitcast.10), calls=%async_computation.2 | async-start | bytes 1835008 | tf_op jit(solution)/shard_map/all_to_all | solution.py:318
  90.8 0.8 slice_bitcast_fusion
  91.7 13.2 %all-to-all-done.2 = bf16[16,224,128]{2,1,0:T(8,128)(2,1)S(1)} async-done(((bf16[16,224,128]{2,1,0:T(8,128)(2,1)}), bf16[16,224,128]{2,1,0:T(8,128)(2,1)S(1)}, u32[]{:S(2)}, u32[]{:S(2)}) %all-to-all-start.2) | async-done | bytes 917536 | tf_op jit(solution)/shard_map/all_to_all | solution.py:318
  104.8 10.8 %conditional.3 = (bf16[224,256]{1,0:T(8,128)(2,1)}) conditional(s32[]{:T(128)} %bitcast.1, bf16[224,256]{1,0:T(8,128)(2,1)S(1)} %pad_maximum_fusion, bf16[224,256]{1,0:T(8,128)(2,1)S(1)} %pad_maximum_fusion, bf16[224,256]{1,0:T(8,128)(2,1)S(1)} %pad_maximum_fusion, bf16[224,256]{1,0:T(8,128)(2,1)S(1)} %pad_maximum_fusion, ...), branch_computations={%region_16.17_spmd, %region_17.18_spmd, %region_18.19_spmd, %regio... | conditional | bytes 458800 | solution.py:303
  104.9 5.5 %collective-permute-start.29 = (bf16[224,256]{1,0:T(8,128)(2,1)S(1)}, bf16[224,256]{1,0:T(8,128)(2,1)}, u32[]{:S(2)}, u32[]{:S(2)}) collective-permute-start(bf16[224,256]{1,0:T(8,128)(2,1)S(1)} %param.29), channel_id=1, source_target_pairs={{0,240},{16,224},{32,208},{48,192},{64,176},{80,160},{96,144},{112... | collective-permute-start | bytes 344072 | tf_op jit(solution)/shard_map/cond/branch_14_fun/ppermute | solution.py:301
  110.3 5.3 %collective-permute-done.29 = bf16[224,256]{1,0:T(8,128)(2,1)} collective-permute-done((bf16[224,256]{1,0:T(8,128)(2,1)S(1)}, bf16[224,256]{1,0:T(8,128)(2,1)}, u32[]{:S(2)}, u32[]{:S(2)}) %collective-permute-start.29) | collective-permute-done | bytes 114720 | tf_op jit(solution)/shard_map/cond/branch_14_fun/ppermute | solution.py:301
  115.7 1.3 %convert_reduce_fusion = f32[224,128]{1,0:T(8,128)S(1)} fusion(bf16[16,224,128]{2,1,0:T(8,128)(2,1)} %all-to-all-done.3), kind=kLoop, calls=%fused_computation | loop fusion | flops 831488 | bytes 974848 | tf_op jit(solution)/shard_map/reduce_sum | solution.py:342
  117.0 0.1 convert_reduce_fusion.1
  117.1 1.6 %fusion.3 = (bf16[1,224,128]{2,1,0:T(8,128)(2,1)}, bf16[1,224,128]{2,1,0:T(8,128)(2,1)}) fusion(f32[224,128]{1,0:T(8,128)S(1)} %convert_reduce_fusion, bf16[224,256]{1,0:T(8,128)(2,1)} %get-tuple-element.91, pred[]{:T(512)S(6)} %eq.14, bf16[16,224,128]{2,1,0:T(8,128)(2,1)} %all-to-all-done.3, f32[224,128]{1,0:T(8,128)S(1)} %convert_reduce_fusion.1, ...), kind=kLoop, calls=%fused_computation.11 | loop fusion | flops 286720 | bytes 573441 | tf_op jit(solution)/shard_map/broadcast_in_dim | solution.py:343
  (6 shorter events, 0.1 us)
Async XLA Ops:
  3.0 13.6 %collective-permute-start.14 = (bf16[240,256]{1,0:T(8,128)(2,1)S(1)}, bf16[240,256]{1,0:T(8,128)(2,1)}, u32[]{:S(2)}, u32[]{:S(2)}) collective-permute-start(bf16[240,256]{1,0:T(8,128)(2,1)S(1)} %param.14), channel_id=1, source_target_pairs={{0,240},{16,224},{32,208},{48,192},{64,176},{80,160},{96,144},{112... | collective-permute-start | bytes 368648 | tf_op jit(solution)/shard_map/cond/branch_14_fun/ppermute | solution.py:301
  19.8 24.8 %copy-start.2 = (s32[1,3584]{1,0:T(1,128)S(1)}, s32[1,3584]{1,0:T(1,128)}, u32[]{:S(2)}) copy-start(s32[1,3584]{1,0:T(1,128)} %param.40) | copy-start | bytes 43012
  19.8 24.8 %copy-start.1 = (bf16[1,224,1024]{2,1,0:T(8,128)(2,1)S(1)}, bf16[1,224,1024]{2,1,0:T(8,128)(2,1)}, u32[]{:S(2)}) copy-start(bf16[1,224,1024]{2,1,0:T(8,128)(2,1)} %param.36) | copy-start | bytes 1376260
  19.8 20.0 %all-to-all-start = ((bf16[16,224,128]{2,1,0:T(8,128)(2,1)}), bf16[16,224,128]{2,1,0:T(8,128)(2,1)S(1)}, u32[]{:S(2)}, u32[]{:S(2)}) async-start(bf16[16,224,128]{2,1,0:T(8,128)(2,1)} %get-tuple-element.89), calls=%async_computation | async-start | bytes 1835008 | tf_op jit(solution)/shard_map/all_to_all | solution.py:318
  39.8 18.7 %all-to-all-start.1 = ((bf16[16,224,128]{2,1,0:T(8,128)(2,1)}), bf16[16,224,128]{2,1,0:T(8,128)(2,1)S(1)}, u32[]{:S(2)}, u32[]{:S(2)}) async-start(bf16[16,224,128]{2,1,0:T(8,128)(2,1)} %get-tuple-element.88), calls=%async_computation.1 | async-start | bytes 1835008 | tf_op jit(solution)/shard_map/all_to_all | solution.py:318
  44.6 14.0 %copy-start = (bf16[1,224,1024]{2,1,0:T(8,128)(2,1)S(1)}, bf16[1,224,1024]{2,1,0:T(8,128)(2,1)}, u32[]{:S(2)}) copy-start(bf16[1,224,1024]{2,1,0:T(8,128)(2,1)} %param.39) | copy-start | bytes 1376260
  63.2 22.9 %all-to-all-start.3 = ((bf16[16,224,128]{2,1,0:T(8,128)(2,1)}), bf16[16,224,128]{2,1,0:T(8,128)(2,1)}, u32[]{:S(2)}, u32[]{:S(2)}) async-start(bf16[16,224,128]{2,1,0:T(8,128)(2,1)} %bitcast.12), calls=%async_computation.3 | async-start | bytes 1835008 | tf_op jit(solution)/shard_map/all_to_all | solution.py:318
  86.1 18.7 %all-to-all-start.2 = ((bf16[16,224,128]{2,1,0:T(8,128)(2,1)}), bf16[16,224,128]{2,1,0:T(8,128)(2,1)S(1)}, u32[]{:S(2)}, u32[]{:S(2)}) async-start(bf16[16,224,128]{2,1,0:T(8,128)(2,1)} %bitcast.10), calls=%async_computation.2 | async-start | bytes 1835008 | tf_op jit(solution)/shard_map/all_to_all | solution.py:318
  104.9 10.8 %collective-permute-start.29 = (bf16[224,256]{1,0:T(8,128)(2,1)S(1)}, bf16[224,256]{1,0:T(8,128)(2,1)}, u32[]{:S(2)}, u32[]{:S(2)}) collective-permute-start(bf16[224,256]{1,0:T(8,128)(2,1)S(1)} %param.29), channel_id=1, source_target_pairs={{0,240},{16,224},{32,208},{48,192},{64,176},{80,160},{96,144},{112... | collective-permute-start | bytes 344072 | tf_op jit(solution)/shard_map/cond/branch_14_fun/ppermute | solution.py:301
